TPU v7x, 512 devices: a whole 4x4x16 slice. The times are simulated.
512 devices in a mesh: enc: 16 (over x, z_hi), seq: 8 (over y, core), tp: 4 (over z_lo).
Axes of the slice: x: 4, y: 4, z: 16 (z_hi: 4, z_lo: 4; z = z_hi * 4 + z_lo), core: 2. Of those that a mesh axis runs over, the one named last changes fastest.
Arguments:
- visual_key_value: bfloat16 [16, 16, 256, 2048], P(None, 'seq', 'enc', 'tp'), may hold values from -4.5 to 4.5
- patch_blocks: int32 [16, 16], P('enc'), may hold values from 1 to 8
- queries: bfloat16 [16, 16, 32, 8192], P('enc', 'seq', None, 'tp'), may hold values from -113 to 113
- suffix_key_value: bfloat16 [16, 16, 32, 2048], P('enc', 'seq', None, 'tp'), may hold values from -6 to 6
- suffix_hidden_state: bfloat16 [16, 16, 32, 8192], P('enc', 'seq', None, 'tp'), may hold values from -6 to 6
- down_weight: bfloat16 [8192, 128], P('tp'), may hold values from -0.0625 to 0.0625
- up_weight: bfloat16 [128, 8192], P(None, 'tp'), may hold values from -1.5 to 1.5
- question_adapter: int32 [16, 16], P('enc', 'seq'), may hold values from 0 to 7
- suffix_token_length: int32 [16, 16], P('enc', 'seq'), may hold values from 1 to 32
Outputs:
- context: bfloat16 [16, 16, 32, 8192], P('enc', 'seq', None, 'tp')
All inputs are finite; a program needn't handle non-finite values.
Results may differ from a plain program's by a relative error of at most 0.0087.
Values may be sent and summed in bfloat16 or wider, within the bound.
A program may use at most 64 MiB of HBM per device.

v0:
```python
import math
import jax
import jax.numpy as jnp
from jax import lax
from jax.sharding import PartitionSpec as P

HEAD_SIZE = 128
ADAPTER_RANK = 16
NEG_BIG = -1e30
ADAPTER_SCALE = 2.0


def sent_to_all(shard, axis):
    copies = jnp.broadcast_to(shard, (lax.axis_size(axis), *shard.shape))
    return lax.all_to_all(copies, axis, split_axis=0, concat_axis=0, tiled=True)


def over_copies(shard, axis):
    return sent_to_all(shard, axis).sum(axis=0)


def per_device(
    visual_key_value,
    patch_blocks,
    queries,
    suffix_key_value,
    suffix_hidden_state,
    down_weight,
    up_weight,
    question_adapter,
    suffix_token_length,
):
    docs_here, asked_here, suffix_len, query_feature_width = queries.shape
    kv_local = suffix_key_value.shape[3] // (2 * HEAD_SIZE)
    head_group = query_feature_width // (kv_local * HEAD_SIZE)
    asked_rows = asked_here * suffix_len
    row_totals = docs_here * asked_rows
    inverse = 1.0 / math.sqrt(HEAD_SIZE)
    enc_count = lax.axis_size("enc")
    hidden_state_rows = suffix_hidden_state.reshape(row_totals, suffix_hidden_state.shape[3])
    reduced_features = jnp.dot(hidden_state_rows, down_weight, preferred_element_type=jnp.float32)
    owning_question = lax.broadcasted_iota(jnp.int32, (1, down_weight.shape[1]), 1) // ADAPTER_RANK
    row_ids = jnp.broadcast_to(
        question_adapter[:, :, None], (docs_here, asked_here, suffix_len)
    ).reshape(row_totals, 1)
    reduced_features = jnp.where(owning_question == row_ids, reduced_features, 0.0)
    selected_adapter = over_copies(reduced_features, "tp").astype(jnp.bfloat16)
    raised_features = jnp.dot(selected_adapter, up_weight, preferred_element_type=jnp.float32)
    query_matrix = (
        queries.reshape(row_totals, query_feature_width).astype(jnp.float32)
        + ADAPTER_SCALE * raised_features
    ).astype(jnp.bfloat16)
    query_matrix = query_matrix.reshape(docs_here, asked_rows, kv_local, head_group, HEAD_SIZE)
    suffix_pairs = suffix_key_value.reshape(
        docs_here, asked_here, suffix_len, kv_local, 2, HEAD_SIZE
    )
    query_split = query_matrix.reshape(
        docs_here, asked_here, suffix_len, kv_local, head_group, HEAD_SIZE
    )
    suffix_scores = (
        jnp.einsum(
            "bqikgd,bqjkd->bkgqij",
            query_split,
            suffix_pairs[:, :, :, :, 0, :],
            preferred_element_type=jnp.float32,
        )
        * inverse
    )
    positions = lax.broadcasted_iota(jnp.int32, (suffix_len, suffix_len), 0)
    columns = lax.broadcasted_iota(jnp.int32, (suffix_len, suffix_len), 1)
    causal = columns <= positions
    within = (
        lax.broadcasted_iota(jnp.int32, (1, 1, suffix_len), 2) < suffix_token_length[:, :, None]
    )
    suffix_mask = (causal[None, None, :, :] & within[:, :, None, :])[:, None, None]
    suffix_scores = jnp.where(suffix_mask, suffix_scores, NEG_BIG)
    suffix_peak = suffix_scores.max(axis=-1)
    suffix_weights = jnp.where(suffix_mask, jnp.exp(suffix_scores - suffix_peak[..., None]), 0.0)
    running = suffix_peak.reshape(docs_here, kv_local, head_group, asked_rows)
    totals = suffix_weights.sum(axis=-1).reshape(docs_here, kv_local, head_group, asked_rows)
    numerators = jnp.einsum(
        "bkgqij,bqjkd->bkgqid",
        suffix_weights.astype(jnp.bfloat16),
        suffix_pairs[:, :, :, :, 1, :],
        preferred_element_type=jnp.float32,
    )
    numerators = numerators.reshape(docs_here, kv_local, head_group, asked_rows, HEAD_SIZE)
    carried = (running, totals, numerators)
    exchanged = lax.all_to_all(visual_key_value, "enc", split_axis=0, concat_axis=0, tiled=True)
    key_piece = lax.all_gather(exchanged, "seq", axis=1, tiled=True)
    peaks_now, totals_now, numer_now = carried
    tile_rows, page_count, tile_len, piece_width = key_piece.shape
    key_values = key_piece.reshape(enc_count, docs_here, page_count, tile_len, piece_width)
    key_values = jnp.moveaxis(key_values, 1, 0).reshape(
        docs_here, enc_count * page_count * tile_len, kv_local, 2, HEAD_SIZE
    )
    token_pos = lax.broadcasted_iota(
        jnp.int32, (1, enc_count, 1, tile_len), 1
    ) * tile_len + lax.broadcasted_iota(jnp.int32, (1, enc_count, 1, tile_len), 3)
    live_keys = 8 * token_pos < patch_blocks[:, None, :, None] * (enc_count * tile_len)
    live_keys = live_keys.reshape(docs_here, 1, 1, 1, enc_count * page_count * tile_len)
    scores = (
        jnp.einsum(
            "bnkgd,blkd->bkgnl",
            query_matrix,
            key_values[:, :, :, 0, :],
            preferred_element_type=jnp.float32,
        )
        * inverse
    )
    scores = jnp.where(live_keys, scores, NEG_BIG)
    updated = jnp.maximum(peaks_now, scores.max(axis=-1))
    rescale = jnp.exp(peaks_now - updated)
    weights = jnp.where(live_keys, jnp.exp(scores - updated[..., None]), 0.0)
    totals_next = totals_now * rescale + weights.sum(axis=-1)
    numer_next = numer_now * rescale[..., None] + jnp.einsum(
        "bkgnl,blkd->bkgnd",
        weights.astype(jnp.bfloat16),
        key_values[:, :, :, 1, :],
        preferred_element_type=jnp.float32,
    )
    carried = (updated, totals_next, numer_next)
    running, totals, numerators = carried
    context = numerators / totals[..., None]
    context = jnp.transpose(context, (0, 3, 1, 2, 4)).reshape(
        docs_here, asked_here, suffix_len, query_feature_width
    )
    kept_rows = (
        lax.broadcasted_iota(jnp.int32, (1, 1, suffix_len), 2) < suffix_token_length[:, :, None]
    )
    return jnp.where(kept_rows[:, :, :, None], context, 0.0).astype(jnp.bfloat16)


def solution(mesh):
    placed = (
        P(None, "seq", "enc", "tp"),
        P("enc", None),
        P("enc", "seq", None, "tp"),
        P("enc", "seq", None, "tp"),
        P("enc", "seq", None, "tp"),
        P("tp", None),
        P(None, "tp"),
        P("enc", "seq"),
        P("enc", "seq"),
    )
    return jax.shard_map(
        per_device,
        mesh=mesh,
        in_specs=placed,
        out_specs=P("enc", "seq", None, "tp"),
        check_vma=False,
    )
```

profile of v0, /device:TPU:1, one launch (start us, length us, event | category | flops | bytes accessed | tf_op | source)
XLA Modules:
  0.0 128.2 jit_solution(13732557373285925791)
XLA Ops:
  6.5 0.0 copy-start
  6.5 0.0 all-gather.2.cloned.1.call-start
  6.5 45.5 %all_to_all.10 = bf16[16,2,16,512]{3,2,1,0:T(8,128)(2,1)} all-to-all(bf16[16,2,16,512]{3,2,1,0:T(8,128)(2,1)} %param.9), channel_id=1, replica_groups=mesh['enc'=16,'seq'=8,'tp'=4] {'enc'}, dimensions={0} | all-to-all | bytes 1048576 | tf_op jit(solution)/shard_map/all_to_all | solution.py:89
  52.1 0.0 all-gather.2.cloned.1.call-update
  52.1 0.7 broadcast_in_dim.81
  52.8 0.1 broadcast_in_dim.82
  52.9 1.3 %convolution_select_fusion = f32[64,128]{1,0:T(8,128)S(1)} fusion(bf16[64,2048]{1,0:T(8,128)(2,1)} %bitcast.147, bf16[2048,128]{1,0:T(8,128)(2,1)} %param.14, s32[128]{0:T(128)S(1)} %and_select_fusion, s32[64]{0:T(128)S(1)} %broadcast_in_dim.82), kind=kOutput, calls=%fused_computation.24 | convolution fusion | flops 33570816 | bytes 819968 | tf_op jit(solution)/shard_map/dot_general | solution.py:41
  54.3 0.7 broadcast_in_dim.84
  54.9 9.1 %all-to-all-start = ((f32[4,64,128]{2,1,0:T(8,128)}), f32[4,64,128]{2,1,0:T(8,128)S(1)}, u32[]{:S(2)}, u32[]{:S(2)}) async-start(f32[4,64,128]{2,1,0:T(8,128)} %broadcast_in_dim.84), calls=%async_computation | async-start | bytes 262144 | tf_op jit(solution)/shard_map/all_to_all | solution.py:15
  64.0 0.7 multiply_bitcast_fusion
  64.7 0.1 add_multiply_fusion
  64.8 0.1 broadcast_compare_fusion
  64.9 0.1 lt.61
  65.0 0.9 reshape.308
  65.9 0.7 iota_compare_fusion.1
  66.6 0.1 fusion.39
  66.7 2.1 %all-to-all-done = f32[4,64,128]{2,1,0:T(8,128)S(1)} async-done(((f32[4,64,128]{2,1,0:T(8,128)}), f32[4,64,128]{2,1,0:T(8,128)S(1)}, u32[]{:S(2)}, u32[]{:S(2)}) %all-to-all-start) | async-done | bytes 131104 | tf_op jit(solution)/shard_map/all_to_all | solution.py:15
  68.8 0.0 copy-done
  68.8 1.2 fusion.17
  70.1 0.4 fusion.40
  70.4 0.4 fusion.25
  70.8 0.2 convolution_bitcast_fusion
  71.1 19.3 %all-gather.2.cloned.1.call-done = bf16[16,16,16,512]{3,2,1,0:T(8,128)(2,1)} async-done(((bf16[16,2,16,512]{3,2,1,0:T(8,128)(2,1)}), bf16[16,16,16,512]{3,2,1,0:T(8,128)(2,1)}) %all-gather.2.cloned.1.call-update) | async-done | bytes 4194320 | tf_op jit(solution)/shard_map/all_gather | solution.py:90
  90.3 6.9 %reshape_transpose_reshape.3 = bf16[1,4096,2,2,128]{4,3,2,1,0:T(2,128)(2,1)} reshape(bf16[16,16,16,512]{3,2,1,0:T(8,128)(2,1)} %all-gather.2.cloned.1.call-done) | data formatting | bytes 8388608 | tf_op jit(solution)/shard_map/reshape;transpose;reshape | solution.py:94
  97.2 9.0 %fusion.38 = (bf16[1,4096,2,1,128]{4,3,2,1,0:T(2,128)(2,1)S(1)}, bf16[1,4096,2,1,128]{4,3,2,1,0:T(2,128)(2,1)S(1)}) fusion(bf16[1,4096,2,2,128]{4,3,2,1,0:T(2,128)(2,1)} %reshape_transpose_reshape.3), kind=kLoop, calls=%fused_computation.56 | loop fusion | bytes 8388608 | tf_op jit(solution)/shard_map/slice | solution.py:106
  106.2 2.9 %fusion.1 = (f32[2,8,64]{1,2,0:T(8,128)S(1)}, f32[2,64,8,4096]{3,2,1,0:T(8,128)S(1)}) fusion(pred[4096]{0:T(1024)(128)(4,1)S(1)} %lt.61, bf16[1,4096,2,1,128]{4,3,2,1,0:T(2,128)(2,1)S(1)} %get-tuple-element.7, bf16[64,2,8,128]{3,2,1,0:T(8,128)(2,1)S(1)} %bitcast.143), kind=kOutput, calls=%fused_computation.3 | convolution fusion | flops 1086323712 | bytes 19144704 | tf_op jit(solution)/shard_map/bnkgd,blkd->bkgnl/dot_general | solution.py:103
  109.2 4.9 %fusion.2 = f32[2,8,64]{1,2,0:T(8,128)S(1)} fusion(f32[2,64,8,4096]{3,2,1,0:T(8,128)S(1)} %get-tuple-element.16, f32[2,8,64]{1,2,0:T(8,128)S(1)} %max.17, pred[4096]{0:T(1024)(128)(4,1)S(1)} %lt.61), kind=kLoop, calls=%fused_computation.4 | loop fusion | flops 20970496 | bytes 16789504 | tf_op jit(solution)/shard_map/reduce_sum | solution.py:115
  114.1 4.8 %fusion.21 = f32[1,64,2,8,128]{4,3,1,2,0:T(8,128)} fusion(bf16[1,4096,2,1,128]{4,3,2,1,0:T(2,128)(2,1)S(1)} %get-tuple-element.8, f32[2,64,8,4096]{3,2,1,0:T(8,128)S(1)} %get-tuple-element.16, f32[2,8,64]{1,2,0:T(8,128)S(1)} %max.17, pred[4096]{0:T(1024)(128)(4,1)S(1)} %lt.61, f32[2,8,64,128]{3,2,1,0:T(8,128)S(1)} %bitcast.146, ...), kind=kOutput, calls=%fused_computation.23 | convolution fusion | flops 1095106560 | bytes 19939328 | tf_op jit(solution)/shard_map/bkgnl,blkd->bkgnd/dot_general | solution.py:116
  118.9 1.1 copy.38
  120.0 0.5 fusion.24
  120.5 0.9 copy.39
  (9 shorter events, 0.1 us)
Async XLA Ops:
  6.5 62.3 %copy-start = (bf16[128,2048]{1,0:T(8,128)(2,1)S(1)}, bf16[128,2048]{1,0:T(8,128)(2,1)}, u32[]{:S(2)}) copy-start(bf16[128,2048]{1,0:T(8,128)(2,1)} %param.15) | copy-start | bytes 1572868
  6.5 83.8 %all-gather.2.cloned.1.call-start = ((), (), s32[]{:S(2)}) async-start(), calls=%async_computation.2 | async-start | bytes 4718592 | tf_op jit(solution)/shard_map/all_gather | solution.py:90
  54.9 13.9 %all-to-all-start = ((f32[4,64,128]{2,1,0:T(8,128)}), f32[4,64,128]{2,1,0:T(8,128)S(1)}, u32[]{:S(2)}, u32[]{:S(2)}) async-start(f32[4,64,128]{2,1,0:T(8,128)} %broadcast_in_dim.84), calls=%async_computation | async-start | bytes 262144 | tf_op jit(solution)/shard_map/all_to_all | solution.py:15
Sparse Core Ops, SparseCore 0:
  52.2 38.0 all-gather.1
where the time goes:
time: 129 us; the launch traced here: 128 us
  blocking collectives  45.5 us (35%)
  waiting for transfers between devices  21.4 us (17%)
  local copies, waits for them, and re-layouts  20.4 us (16%)
  between operations  13.5 us (10%)
  matrix products  10.8 us (8%)
  starting transfers between devices  9.1 us (7%)
  other arithmetic  7.44 us (6%)
    all_to_all x1, blocking collectives, per_device(): lax.all_to_all(visual_key_value, 'enc', split_axis=0, concat_axis=0, tile...  45.5 us
    all_gather x1, waiting for transfers between devices, per_device(): key_piece = lax.all_gather(exchanged, 'seq', axis=1, tiled=True)  19.3 us
    all_to_all x1, starting transfers between devices, sent_to_all(): return lax.all_to_all(copies, axis, split_axis=0, concat_axis=0, tiled=True)  9.1 us
    slice x1, local copies, waits for them, and re-layouts, per_device(): key_values[:, :, :, 0, :]  8.97 us
    another operation x1, local copies, waits for them, and re-layouts, per_device(): jnp.moveaxis(key_values, 1, 0)  6.92 us
    reduce_sum x1, other arithmetic, per_device(): totals_next = totals_now * rescale + weights.sum(axis=-1)  4.91 us
    dot_general x1, matrix products, per_device(): jnp.einsum('bkgnl,blkd->bkgnd', weights.astype(jnp.bfloat16), key_values[...  4.77 us
    dot_general x1, matrix products, per_device(): jnp.einsum('bnkgd,blkd->bkgnl', query_matrix, key_values[:, :, :, 0, :],...  2.92 us
  transfers between devices with their start and end apart: 2, of which 2 were waited for; matrix products, arithmetic and copies ran while one was open for 6% of the time, Pallas kernels for 0%

commit v1 on v0

--- a/solution.py
+++ b/solution.py
@@ -8,6 +8,17 @@
 ADAPTER_RANK = 16
 NEG_BIG = -1e30
 ADAPTER_SCALE = 2.0
+
+
+def around_the_ring(shard, axis, dim):
+    size = lax.axis_size(axis)
+    right = [(i, (i + 1) % size) for i in range(size)]
+    parts = [shard]
+    for reach in range(1, size):
+        parts = [lax.ppermute(parts[0], axis, right), *parts]
+    whole = jnp.concatenate(parts, axis=dim)
+    turn = (lax.axis_index(axis) + 1) * parts[-1].shape[dim]
+    return jnp.roll(whole, turn, axis=dim)
 
 
 def sent_to_all(shard, axis):
@@ -87,7 +98,7 @@
     numerators = numerators.reshape(docs_here, kv_local, head_group, asked_rows, HEAD_SIZE)
     carried = (running, totals, numerators)
     exchanged = lax.all_to_all(visual_key_value, "enc", split_axis=0, concat_axis=0, tiled=True)
-    key_piece = lax.all_gather(exchanged, "seq", axis=1, tiled=True)
+    key_piece = around_the_ring(exchanged, "seq", 1)
     peaks_now, totals_now, numer_now = carried
     tile_rows, page_count, tile_len, piece_width = key_piece.shape
     key_values = key_piece.reshape(enc_count, docs_here, page_count, tile_len, piece_width)

time: 129 us -> 162 us (1.26)
  the two profiles are of different devices: /device:TPU:1 before, /device:TPU:32 now
where the time goes in v1:
time: 162 us; the launch traced here: 161 us
  waiting for transfers between devices  55.3 us (34%)
  blocking collectives  51 us (31%)
  local copies, waits for them, and re-layouts  31.7 us (20%)
  matrix products  12 us (7%)
  other arithmetic  7.41 us (5%)
  starting transfers between devices  3.74 us (2%)
    ppermute x7, waiting for transfers between devices, around_the_ring(): parts = [lax.ppermute(parts[0], axis, right), *parts]  55.3 us
    all_to_all x1, blocking collectives, per_device(): lax.all_to_all(visual_key_value, 'enc', split_axis=0, concat_axis=0, tile...  51 us
    slice x1, local copies, waits for them, and re-layouts, per_device(): key_values[:, :, :, 0, :]  8.9 us
    unnamed x24, local copies, waits for them, and re-layouts  8.65 us
    another operation x1, local copies, waits for them, and re-layouts, per_device(): jnp.moveaxis(key_values, 1, 0)  6.94 us
    reduce_sum x1, other arithmetic, per_device(): totals_next = totals_now * rescale + weights.sum(axis=-1)  4.9 us
    dot_general x1, matrix products, per_device(): jnp.einsum('bnkgd,blkd->bkgnl', query_matrix, key_values[:, :, :, 0, :],...  4.11 us
    dot_general x1, matrix products, per_device(): jnp.einsum('bkgnl,blkd->bkgnd', weights.astype(jnp.bfloat16), key_values[...  3.81 us
  transfers between devices with their start and end apart: 8, of which 7 were waited for; matrix products, arithmetic and copies ran while one was open for 6% of the time, Pallas kernels for 0%

profile of v1, /device:TPU:32, one launch (start us, length us, event | category | flops | bytes accessed | tf_op | source)
XLA Modules:
  0.0 161.4 jit_solution(14178566122234080584)
XLA Ops:
  0.0 0.0 copy-start
  0.0 51.0 %all_to_all.10 = bf16[16,2,16,512]{3,2,1,0:T(8,128)(2,1)S(1)} all-to-all(bf16[16,2,16,512]{3,2,1,0:T(8,128)(2,1)} %param.9), channel_id=1, replica_groups=mesh['enc'=16,'seq'=8,'tp'=4] {'enc'}, dimensions={0} | all-to-all | bytes 1048576 | tf_op jit(solution)/shard_map/all_to_all | solution.py:100
  51.0 0.0 collective-permute-start
  51.0 9.8 %collective-permute-done = bf16[16,2,16,512]{3,2,1,0:T(8,128)(2,1)S(1)} collective-permute-done((bf16[16,2,16,512]{3,2,1,0:T(8,128)(2,1)S(1)}, bf16[16,2,16,512]{3,2,1,0:T(8,128)(2,1)S(1)}, u32[]{:S(2)}, u32[]{:S(2)}) %collective-permute-start) | collective-permute-done | bytes 524320 | tf_op jit(solution)/shard_map/ppermute | solution.py:18
  60.8 0.0 collective-permute-start.1
  60.8 9.8 %collective-permute-done.1 = bf16[16,2,16,512]{3,2,1,0:T(8,128)(2,1)S(1)} collective-permute-done((bf16[16,2,16,512]{3,2,1,0:T(8,128)(2,1)S(1)}, bf16[16,2,16,512]{3,2,1,0:T(8,128)(2,1)S(1)}, u32[]{:S(2)}, u32[]{:S(2)}) %collective-permute-start.1) | collective-permute-done | bytes 524320 | tf_op jit(solution)/shard_map/ppermute | solution.py:18
  70.7 0.0 collective-permute-start.2
  70.7 0.7 broadcast_in_dim.81
  71.4 0.1 broadcast_in_dim.82
  71.5 1.3 convolution_select_fusion
  72.8 0.7 broadcast_in_dim.84
  73.5 3.7 %all-to-all-start = ((f32[4,64,128]{2,1,0:T(8,128)}), f32[4,64,128]{2,1,0:T(8,128)S(1)}, u32[]{:S(2)}, u32[]{:S(2)}) async-start(f32[4,64,128]{2,1,0:T(8,128)} %broadcast_in_dim.84), calls=%async_computation | async-start | bytes 262144 | tf_op jit(solution)/shard_map/all_to_all | solution.py:26
  77.2 3.3 %collective-permute-done.2 = bf16[16,2,16,512]{3,2,1,0:T(8,128)(2,1)S(1)} collective-permute-done((bf16[16,2,16,512]{3,2,1,0:T(8,128)(2,1)S(1)}, bf16[16,2,16,512]{3,2,1,0:T(8,128)(2,1)S(1)}, u32[]{:S(2)}, u32[]{:S(2)}) %collective-permute-start.2) | collective-permute-done | bytes 524320 | tf_op jit(solution)/shard_map/ppermute | solution.py:18
  80.5 0.0 collective-permute-start.3
  80.5 0.7 multiply_bitcast_fusion
  81.1 0.1 add_multiply_fusion
  81.2 9.1 %collective-permute-done.3 = bf16[16,2,16,512]{3,2,1,0:T(8,128)(2,1)S(1)} collective-permute-done((bf16[16,2,16,512]{3,2,1,0:T(8,128)(2,1)S(1)}, bf16[16,2,16,512]{3,2,1,0:T(8,128)(2,1)S(1)}, u32[]{:S(2)}, u32[]{:S(2)}) %collective-permute-start.3) | collective-permute-done | bytes 524320 | tf_op jit(solution)/shard_map/ppermute | solution.py:18
  90.3 0.0 copy-start.1
  90.3 0.0 collective-permute-start.4
  90.3 0.1 broadcast_compare_fusion
  90.4 0.1 lt.73
  90.5 0.9 reshape.308
  91.4 0.7 iota_compare_fusion.1
  92.1 8.1 %collective-permute-done.4 = bf16[16,2,16,512]{3,2,1,0:T(8,128)(2,1)} collective-permute-done((bf16[16,2,16,512]{3,2,1,0:T(8,128)(2,1)S(1)}, bf16[16,2,16,512]{3,2,1,0:T(8,128)(2,1)}, u32[]{:S(2)}, u32[]{:S(2)}) %collective-permute-start.4) | collective-permute-done | bytes 524320 | tf_op jit(solution)/shard_map/ppermute | solution.py:18
  100.2 0.0 collective-permute-start.5
  100.2 0.1 fusion.36
  100.3 0.0 all-to-all-done
  100.4 0.0 copy-done
  100.4 1.2 fusion.17
  101.6 0.7 copy.61
  102.3 8.0 %collective-permute-done.5 = bf16[16,2,16,512]{3,2,1,0:T(8,128)(2,1)} collective-permute-done((bf16[16,2,16,512]{3,2,1,0:T(8,128)(2,1)}, bf16[16,2,16,512]{3,2,1,0:T(8,128)(2,1)}, u32[]{:S(2)}, u32[]{:S(2)}) %collective-permute-start.5) | collective-permute-done | bytes 524320 | tf_op jit(solution)/shard_map/ppermute | solution.py:18
  110.3 0.0 collective-permute-start.6
  110.3 0.0 copy-done.1
  110.4 1.3 fusion.37
  111.7 0.1 copy.48
  111.7 0.4 fusion.25
  112.1 0.0 copy-start.2
  112.1 0.2 convolution_bitcast_fusion
  112.4 0.9 copy.44
  113.2 0.1 copy.50
  113.3 7.2 %collective-permute-done.6 = bf16[16,2,16,512]{3,2,1,0:T(8,128)(2,1)} collective-permute-done((bf16[16,2,16,512]{3,2,1,0:T(8,128)(2,1)}, bf16[16,2,16,512]{3,2,1,0:T(8,128)(2,1)}, u32[]{:S(2)}, u32[]{:S(2)}) %collective-permute-start.6) | collective-permute-done | bytes 524320 | tf_op jit(solution)/shard_map/ppermute | solution.py:18
  120.5 1.1 constant_dynamic-update-slice_fusion.15
  121.6 1.1 constant_dynamic-update-slice_fusion.14
  122.7 1.1 constant_dynamic-update-slice_fusion.13
  123.7 1.1 constant_dynamic-update-slice_fusion.12
  125.0 1.1 constant_dynamic-update-slice_fusion.7
  126.1 1.1 constant_dynamic-update-slice_fusion.6
  127.2 1.1 constant_dynamic-update-slice_fusion.5
  128.3 0.0 copy-done.2
  128.5 2.4 %constant_dynamic-slice_fusion = bf16[16,16,16,512]{3,2,1,0:T(8,128)(2,1)} fusion(bf16[16,32,16,512]{3,2,1,0:T(8,128)(2,1)S(1)} %constant_dynamic-update-slice_fusion, s32[]{:T(128)S(6)} %select_n.61), kind=kLoop, calls=%fused_computation.67 | loop fusion | bytes 8388612 | tf_op jit(solution)/shard_map/jit(_roll_dynamic)/dynamic_slice | solution.py:21
  131.0 6.9 %reshape_transpose_reshape.3 = bf16[1,4096,2,2,128]{4,3,2,1,0:T(2,128)(2,1)} reshape(bf16[16,16,16,512]{3,2,1,0:T(8,128)(2,1)} %constant_dynamic-slice_fusion) | data formatting | bytes 8388608 | tf_op jit(solution)/shard_map/reshape;transpose;reshape | solution.py:105
  137.9 8.9 %fusion.35 = (bf16[1,4096,2,1,128]{4,3,2,1,0:T(2,128)(2,1)S(1)}, bf16[1,4096,2,1,128]{4,3,2,1,0:T(2,128)(2,1)S(1)}) fusion(bf16[1,4096,2,2,128]{4,3,2,1,0:T(2,128)(2,1)} %reshape_transpose_reshape.3), kind=kLoop, calls=%fused_computation.71 | loop fusion | bytes 8388608 | tf_op jit(solution)/shard_map/slice | solution.py:117
  146.8 4.1 %bitcast_reduce_fusion = (f32[2,8,64]{2,1,0:T(8,128)S(1)}, f32[2,4096,64,8]{1,2,3,0:T(8,128)S(1)}) fusion(pred[4096]{0:T(1024)(128)(4,1)S(1)} %lt.73, bf16[64,2,8,128]{3,2,1,0:T(8,128)(2,1)} %bitcast.54, bf16[1,4096,2,1,128]{4,3,2,1,0:T(2,128)(2,1)S(1)} %get-tuple-element.7), kind=kOutput, calls=%fused_computation.1 | convolution fusion | flops 1086323712 | bytes 19144704 | tf_op jit(solution)/shard_map/bnkgd,blkd->bkgnl/dot_general | solution.py:114
  150.9 0.0 copy-start.3
  151.0 4.9 %fusion.2 = f32[2,8,64]{2,1,0:T(8,128)S(1)} fusion(f32[2,4096,64,8]{1,2,3,0:T(8,128)S(1)} %get-tuple-element.16, f32[2,8,64]{2,1,0:T(8,128)S(1)} %max.17, pred[4096]{0:T(1024)(128)(4,1)S(1)} %lt.73), kind=kLoop, calls=%fused_computation.5 | loop fusion | flops 20970496 | bytes 16789504 | tf_op jit(solution)/shard_map/reduce_sum | solution.py:126
  155.9 0.0 copy-done.3
  155.9 3.8 %fusion.21 = f32[1,64,2,8,128]{4,1,3,2,0:T(8,128)S(1)} fusion(bf16[1,4096,2,1,128]{4,3,2,1,0:T(2,128)(2,1)S(1)} %get-tuple-element.8, f32[2,4096,64,8]{1,2,3,0:T(8,128)S(1)} %get-tuple-element.16, f32[2,8,64]{2,1,0:T(8,128)S(1)} %max.17, pred[4096]{0:T(1024)(128)(4,1)S(1)} %lt.73, f32[2,8,64,128]{3,2,1,0:T(8,128)S(1)} %bitcast.134, ...), kind=kOutput, calls=%fused_computation.24 | convolution fusion | flops 1095106560 | bytes 19939328 | tf_op jit(solution)/shard_map/bkgnl,blkd->bkgnd/dot_general | solution.py:127
  159.7 0.3 copy.51
  160.0 0.5 fusion.24
  160.5 0.9 copy.52
  (16 shorter events, 0.4 us)
Async XLA Ops:
  0.0 100.4 %copy-start = (bf16[128,2048]{1,0:T(8,128)(2,1)S(1)}, bf16[128,2048]{1,0:T(8,128)(2,1)}, u32[]{:S(2)}) copy-start(bf16[128,2048]{1,0:T(8,128)(2,1)} %param.15) | copy-start | bytes 1572868
  51.0 9.8 %collective-permute-start = (bf16[16,2,16,512]{3,2,1,0:T(8,128)(2,1)S(1)}, bf16[16,2,16,512]{3,2,1,0:T(8,128)(2,1)S(1)}, u32[]{:S(2)}, u32[]{:S(2)}) collective-permute-start(bf16[16,2,16,512]{3,2,1,0:T(8,128)(2,1)S(1)} %all_to_all.10), channel_id=1, source_target_pairs={{0,4},{4,8},{8,12},{12,16},{16,20},{20,24},{24,28},{28,0},{1,5},{5... | collective-permute-start | bytes 1572872 | tf_op jit(solution)/shard_map/ppermute | solution.py:18
  60.8 9.8 %collective-permute-start.1 = (bf16[16,2,16,512]{3,2,1,0:T(8,128)(2,1)S(1)}, bf16[16,2,16,512]{3,2,1,0:T(8,128)(2,1)S(1)}, u32[]{:S(2)}, u32[]{:S(2)}) collective-permute-start(bf16[16,2,16,512]{3,2,1,0:T(8,128)(2,1)S(1)} %collective-permute-done), channel_id=1, source_target_pairs={{0,4},{4,8},{8,12},{12,16},{16,20},{20,24},{24,28},{28,0},{1,5},{5... | collective-permute-start | bytes 1572872 | tf_op jit(solution)/shard_map/ppermute | solution.py:18
  70.7 9.8 %collective-permute-start.2 = (bf16[16,2,16,512]{3,2,1,0:T(8,128)(2,1)S(1)}, bf16[16,2,16,512]{3,2,1,0:T(8,128)(2,1)S(1)}, u32[]{:S(2)}, u32[]{:S(2)}) collective-permute-start(bf16[16,2,16,512]{3,2,1,0:T(8,128)(2,1)S(1)} %collective-permute-done.1), channel_id=1, source_target_pairs={{0,4},{4,8},{8,12},{12,16},{16,20},{20,24},{24,28},{28,0},{1,5},{5... | collective-permute-start | bytes 1572872 | tf_op jit(solution)/shard_map/ppermute | solution.py:18
  73.5 26.8 %all-to-all-start = ((f32[4,64,128]{2,1,0:T(8,128)}), f32[4,64,128]{2,1,0:T(8,128)S(1)}, u32[]{:S(2)}, u32[]{:S(2)}) async-start(f32[4,64,128]{2,1,0:T(8,128)} %broadcast_in_dim.84), calls=%async_computation | async-start | bytes 262144 | tf_op jit(solution)/shard_map/all_to_all | solution.py:26
  80.5 9.8 %collective-permute-start.3 = (bf16[16,2,16,512]{3,2,1,0:T(8,128)(2,1)S(1)}, bf16[16,2,16,512]{3,2,1,0:T(8,128)(2,1)S(1)}, u32[]{:S(2)}, u32[]{:S(2)}) collective-permute-start(bf16[16,2,16,512]{3,2,1,0:T(8,128)(2,1)S(1)} %collective-permute-done.2), channel_id=1, source_target_pairs={{0,4},{4,8},{8,12},{12,16},{16,20},{20,24},{24,28},{28,0},{1,5},{5... | collective-permute-start | bytes 1572872 | tf_op jit(solution)/shard_map/ppermute | solution.py:18
  90.3 20.1 %copy-start.1 = (bf16[16,2,16,512]{3,2,1,0:T(8,128)(2,1)}, bf16[16,2,16,512]{3,2,1,0:T(8,128)(2,1)S(1)}, u32[]{:S(2)}) copy-start(bf16[16,2,16,512]{3,2,1,0:T(8,128)(2,1)S(1)} %collective-permute-done.3) | copy-start | bytes 1572868
  90.3 9.9 %collective-permute-start.4 = (bf16[16,2,16,512]{3,2,1,0:T(8,128)(2,1)S(1)}, bf16[16,2,16,512]{3,2,1,0:T(8,128)(2,1)}, u32[]{:S(2)}, u32[]{:S(2)}) collective-permute-start(bf16[16,2,16,512]{3,2,1,0:T(8,128)(2,1)S(1)} %collective-permute-done.3), channel_id=1, source_target_pairs={{0,4},{4,8},{8,12},{12,16},{16,20},{20,24},{24,28},{28,0},{1,5},{5... | collective-permute-start | bytes 1572872 | tf_op jit(solution)/shard_map/ppermute | solution.py:18
  100.2 10.1 %collective-permute-start.5 = (bf16[16,2,16,512]{3,2,1,0:T(8,128)(2,1)}, bf16[16,2,16,512]{3,2,1,0:T(8,128)(2,1)}, u32[]{:S(2)}, u32[]{:S(2)}) collective-permute-start(bf16[16,2,16,512]{3,2,1,0:T(8,128)(2,1)} %collective-permute-done.4), channel_id=1, source_target_pairs={{0,4},{4,8},{8,12},{12,16},{16,20},{20,24},{24,28},{28,0},{1,5},{5... | collective-permute-start | bytes 1572872 | tf_op jit(solution)/shard_map/ppermute | solution.py:18
  110.3 10.1 %collective-permute-start.6 = (bf16[16,2,16,512]{3,2,1,0:T(8,128)(2,1)}, bf16[16,2,16,512]{3,2,1,0:T(8,128)(2,1)}, u32[]{:S(2)}, u32[]{:S(2)}) collective-permute-start(bf16[16,2,16,512]{3,2,1,0:T(8,128)(2,1)} %collective-permute-done.5), channel_id=1, source_target_pairs={{0,4},{4,8},{8,12},{12,16},{16,20},{20,24},{24,28},{28,0},{1,5},{5... | collective-permute-start | bytes 1572872 | tf_op jit(solution)/shard_map/ppermute | solution.py:18
  112.1 16.2 %copy-start.2 = (bf16[16,2,16,512]{3,2,1,0:T(8,128)(2,1)S(1)}, bf16[16,2,16,512]{3,2,1,0:T(8,128)(2,1)}, u32[]{:S(2)}) copy-start(bf16[16,2,16,512]{3,2,1,0:T(8,128)(2,1)} %copy-done.1) | copy-start | bytes 1572868
  150.9 4.9 %copy-start.3 = (f32[1,2,8,2,32,128]{5,4,3,2,1,0:T(8,128)S(1)}, f32[1,2,8,2,32,128]{5,4,3,2,1,0:T(8,128)}, u32[]{:S(2)}) copy-start(f32[1,2,8,2,32,128]{5,4,3,2,1,0:T(8,128)} %copy.44) | copy-start | bytes 1572868
